TPU v7x, 32 devices: a whole 2x2x4 slice. The times are simulated.
32 devices in a mesh: dp: 4 (over z), fsdp: 8 (over y, x, core).
Axes of the slice: x: 2, y: 2, z: 4, core: 2. Of those that a mesh axis runs over, the one named last changes fastest.
Arguments:
- tokens: bfloat16 [32768, 768], P(('dp', 'fsdp')), may hold values from -6 to 6
- cotangent: bfloat16 [32768, 768], P(('dp', 'fsdp')), may hold values from -6 to 6
- crop_rows: int32 [128], P(('dp', 'fsdp')), may hold values from 12 to 16, as said below
- crop_top: int32 [128], P(('dp', 'fsdp')), may hold values from 0 to 4, as said below
- attn_gain: bfloat16 [768], P('fsdp'), may hold values from 0.5 to 1.5
- attn_shift: bfloat16 [768], P('fsdp'), may hold values from -1.5 to 1.5
- heads_weight: bfloat16 [768, 2304], P('fsdp'), may hold values from -0.3125 to 0.3125
- heads_bias: bfloat16 [1536], P('fsdp'), may hold values from -2.5 to 2.5
- proj_weight: bfloat16 [768, 768], P('fsdp'), may hold values from -0.625 to 0.625
- proj_bias: bfloat16 [768], P('fsdp'), may hold values from -2.5 to 2.5
- mlp_gain: bfloat16 [768], P('fsdp'), may hold values from 0.5 to 1.5
- mlp_shift: bfloat16 [768], P('fsdp'), may hold values from -1.5 to 1.5
- up_weight: bfloat16 [768, 3072], P('fsdp'), may hold values from -0.21875 to 0.21875
- up_bias: bfloat16 [3072], P('fsdp'), may hold values from -2.5 to 2.5
- down_weight: bfloat16 [3072, 768], P('fsdp'), may hold values from -0.15625 to 0.15625
- down_bias: bfloat16 [768], P('fsdp'), may hold values from -2.5 to 2.5
Outputs:
- block_out: bfloat16 [32768, 768], P(('dp', 'fsdp'))
- tokens_grad: bfloat16 [32768, 768], P(('dp', 'fsdp'))
- attn_gain_grad: float32 [768], P('fsdp')
- attn_shift_grad: float32 [768], P('fsdp')
- heads_weight_grad: float32 [768, 2304], P('fsdp')
- heads_bias_grad: float32 [1536], P('fsdp')
- proj_weight_grad: float32 [768, 768], P('fsdp')
- proj_bias_grad: float32 [768], P('fsdp')
- mlp_gain_grad: float32 [768], P('fsdp')
- mlp_shift_grad: float32 [768], P('fsdp')
- up_weight_grad: float32 [768, 3072], P('fsdp')
- up_bias_grad: float32 [3072], P('fsdp')
- down_weight_grad: float32 [3072, 768], P('fsdp')
- down_bias_grad: float32 [768], P('fsdp')
Inputs may be any that keep to these rules, and one draw needn't show every extreme that they name: Image b's crop holds crop_rows[b] whole grid rows of 16 slots each. Image b's crop fills grid rows crop_top[b] to crop_top[b] + crop_rows[b] - 1, all within the 16 rows.
All inputs are finite; a program needn't handle non-finite values.
Results may differ from a plain program's by a relative error of at most 0.019.
Values may be sent and summed in bfloat16 or wider, within the bound.
A program may use at most 192 MiB of HBM per device.

v0:
```python
from functools import partial
import math

import jax
import jax.numpy as jnp
from jax import lax
from jax.sharding import PartitionSpec as P

HEADS = 16


EPSILON = 1e-06
NEGATIVE = -1e30


def layer_norm(entries, norm_gain, norm_shift):
    centered = entries - jnp.mean(entries, axis=-1, keepdims=True)
    spread = jnp.mean(centered * centered, axis=-1, keepdims=True)
    return centered * lax.rsqrt(spread + EPSILON) * norm_gain + norm_shift


def norm_back(entries, norm_gain, norm_shift, upstream):
    result, puller = jax.vjp(layer_norm, entries, norm_gain, norm_shift)
    return puller(upstream)


def gelu_back(hidden, upstream):
    result, puller = jax.vjp(partial(jax.nn.gelu, approximate=True), hidden)
    return puller(upstream)[0]


def masked_scores(queries, key_side, keep_slots):
    scores = jnp.einsum("gihe,gjhe->ghij", queries, key_side, preferred_element_type=jnp.float32)
    return jnp.where(keep_slots[:, None, None, :], scores, NEGATIVE)


def attend_forward(pieces):
    queries, key_side, values, keep_slots = pieces
    masked = masked_scores(queries, key_side, keep_slots)
    highest = jnp.max(masked, axis=-1, keepdims=True)
    powers = jnp.exp(masked - highest)
    totals = jnp.sum(powers, axis=-1, keepdims=True)
    probs_low = (powers / totals).astype(jnp.bfloat16)
    heads_out = jnp.einsum("ghij,gjhe->gihe", probs_low, values, preferred_element_type=jnp.float32)
    return (heads_out.astype(jnp.bfloat16), (highest + jnp.log(totals))[..., 0])


def attend_back(pieces):
    queries, key_side, values, keep_slots, log_total, grad_heads = pieces
    masked = masked_scores(queries, key_side, keep_slots)
    probs = jnp.exp(masked - log_total[..., None])
    grad_probs = jnp.einsum(
        "gihe,gjhe->ghij", grad_heads, values, preferred_element_type=jnp.float32
    )
    inner = jnp.sum(probs * grad_probs, axis=-1, keepdims=True)
    grad_scores = (probs * (grad_probs - inner)).astype(jnp.bfloat16)
    factor = 1.0 / math.sqrt(queries.shape[-1])
    grad_query = (
        jnp.einsum("ghij,gjhe->gihe", grad_scores, key_side, preferred_element_type=jnp.float32)
        * factor
    ).astype(jnp.bfloat16)
    grad_key = jnp.einsum(
        "ghij,gihe->gjhe", grad_scores, queries, preferred_element_type=jnp.float32
    ).astype(jnp.bfloat16)
    grad_value = jnp.einsum(
        "ghij,gihe->gjhe",
        probs.astype(jnp.bfloat16),
        grad_heads,
        preferred_element_type=jnp.float32,
    ).astype(jnp.bfloat16)
    return (grad_query, grad_key, grad_value)


def shards(
    tokens,
    cotangent,
    crop_rows,
    crop_top,
    attn_gain,
    attn_shift,
    heads_weight,
    heads_bias,
    proj_weight,
    proj_bias,
    mlp_gain,
    mlp_shift,
    up_weight,
    up_bias,
    down_weight,
    down_bias,
):
    width = heads_weight.shape[1] // 3
    images = crop_rows.shape[0]
    row_count = tokens.shape[0]
    slots = row_count // images
    grid = math.isqrt(slots)
    group = math.gcd(images, max(1, 512 // slots))
    count = images // group
    block_shape = (count, group, slots, HEADS, width // HEADS)
    grid_row = jnp.arange(slots, dtype=jnp.int32) // grid
    keep_slots = jnp.logical_and(
        grid_row[None, :] >= crop_top[:, None],
        grid_row[None, :] < crop_top[:, None] + crop_rows[:, None],
    )
    keep_rows = keep_slots.reshape(-1, 1)
    keep_groups = keep_slots.reshape(count, group, slots)
    attn_full = (
        lax.all_gather(attn_gain, "fsdp", axis=0, tiled=True),
        lax.all_gather(attn_shift, "fsdp", axis=0, tiled=True),
        lax.all_gather(heads_weight, "fsdp", axis=0, tiled=True),
        lax.all_gather(heads_bias, "fsdp", axis=0, tiled=True),
        lax.all_gather(proj_weight, "fsdp", axis=0, tiled=True),
        lax.all_gather(proj_bias, "fsdp", axis=0, tiled=True),
    )
    entries = tokens.astype(jnp.float32)
    first_gain = attn_full[0].astype(jnp.float32)
    first_shift = attn_full[1].astype(jnp.float32)
    low_one = layer_norm(entries, first_gain, first_shift).astype(jnp.bfloat16)
    projected = jnp.dot(low_one, attn_full[2], preferred_element_type=jnp.float32)
    qv_shift = attn_full[3].astype(jnp.float32)
    factor = 1.0 / math.sqrt(width // HEADS)
    queries = (
        ((projected[:, :width] + qv_shift[:width]) * factor)
        .astype(jnp.bfloat16)
        .reshape(block_shape)
    )
    key_side = projected[:, width : 2 * width].astype(jnp.bfloat16).reshape(block_shape)
    values = (
        (projected[:, 2 * width :] + qv_shift[width:]).astype(jnp.bfloat16).reshape(block_shape)
    )
    heads_out, log_total = lax.map(attend_forward, (queries, key_side, values, keep_groups))
    heads_out = heads_out.reshape(row_count, width)
    resid = entries + (
        jnp.dot(heads_out, attn_full[4], preferred_element_type=jnp.float32)
        + attn_full[5].astype(jnp.float32)
    )
    mlp_full = (
        lax.all_gather(mlp_gain, "fsdp", axis=0, tiled=True),
        lax.all_gather(mlp_shift, "fsdp", axis=0, tiled=True),
        lax.all_gather(up_weight, "fsdp", axis=0, tiled=True),
        lax.all_gather(up_bias, "fsdp", axis=0, tiled=True),
        lax.all_gather(down_weight, "fsdp", axis=0, tiled=True),
        lax.all_gather(down_bias, "fsdp", axis=0, tiled=True),
    )
    second_gain = mlp_full[0].astype(jnp.float32)
    second_shift = mlp_full[1].astype(jnp.float32)
    low_two = layer_norm(resid, second_gain, second_shift).astype(jnp.bfloat16)
    hidden = jnp.dot(low_two, mlp_full[2], preferred_element_type=jnp.float32) + mlp_full[3].astype(
        jnp.float32
    )
    active = jax.nn.gelu(hidden, approximate=True).astype(jnp.bfloat16)
    result = resid + (
        jnp.dot(active, mlp_full[4], preferred_element_type=jnp.float32)
        + mlp_full[5].astype(jnp.float32)
    )
    block_out = jnp.where(keep_rows, result, 0.0).astype(jnp.bfloat16)
    back_mlp = (
        lax.all_gather(mlp_gain, "fsdp", axis=0, tiled=True),
        lax.all_gather(mlp_shift, "fsdp", axis=0, tiled=True),
        lax.all_gather(up_weight, "fsdp", axis=0, tiled=True),
        lax.all_gather(up_bias, "fsdp", axis=0, tiled=True),
        lax.all_gather(down_weight, "fsdp", axis=0, tiled=True),
        lax.all_gather(down_bias, "fsdp", axis=0, tiled=True),
    )
    grad_out = jnp.where(keep_rows, cotangent.astype(jnp.float32), 0.0)
    grad_out_low = grad_out.astype(jnp.bfloat16)
    down_bias_part = jnp.sum(grad_out, axis=0)
    down_weight_part = jnp.einsum(
        "rf,rd->fd", active, grad_out_low, preferred_element_type=jnp.float32
    )
    grad_active = jnp.einsum(
        "rd,fd->rf", grad_out_low, back_mlp[4], preferred_element_type=jnp.float32
    )
    grad_hidden = gelu_back(hidden, grad_active).astype(jnp.bfloat16)
    up_bias_part = jnp.sum(grad_hidden.astype(jnp.float32), axis=0)
    up_weight_part = jnp.einsum(
        "rd,rf->df", low_two, grad_hidden, preferred_element_type=jnp.float32
    )
    grad_two = jnp.einsum("rf,df->rd", grad_hidden, back_mlp[2], preferred_element_type=jnp.float32)
    grad_resid_norm, mlp_gain_part, mlp_shift_part = norm_back(
        resid, back_mlp[0].astype(jnp.float32), back_mlp[1].astype(jnp.float32), grad_two
    )
    grad_resid = grad_out + grad_resid_norm
    mlp_gain_sum, mlp_shift_sum, up_weight_sum, up_bias_sum, down_weight_sum, down_bias_sum = (
        lax.psum_scatter(
            mlp_gain_part.astype(jnp.bfloat16), "fsdp", scatter_dimension=0, tiled=True
        ).astype(jnp.float32),
        lax.psum_scatter(
            mlp_shift_part.astype(jnp.bfloat16), "fsdp", scatter_dimension=0, tiled=True
        ).astype(jnp.float32),
        lax.psum_scatter(
            up_weight_part.astype(jnp.bfloat16), "fsdp", scatter_dimension=0, tiled=True
        ).astype(jnp.float32),
        lax.psum_scatter(
            up_bias_part.astype(jnp.bfloat16), "fsdp", scatter_dimension=0, tiled=True
        ).astype(jnp.float32),
        lax.psum_scatter(
            down_weight_part.astype(jnp.bfloat16), "fsdp", scatter_dimension=0, tiled=True
        ).astype(jnp.float32),
        lax.psum_scatter(
            down_bias_part.astype(jnp.bfloat16), "fsdp", scatter_dimension=0, tiled=True
        ).astype(jnp.float32),
    )
    mlp_gain_sum, mlp_shift_sum, up_weight_sum, up_bias_sum, down_weight_sum, down_bias_sum = (
        lax.psum(mlp_gain_sum.astype(jnp.bfloat16), "dp").astype(jnp.float32),
        lax.psum(mlp_shift_sum.astype(jnp.bfloat16), "dp").astype(jnp.float32),
        lax.psum(up_weight_sum.astype(jnp.bfloat16), "dp").astype(jnp.float32),
        lax.psum(up_bias_sum.astype(jnp.bfloat16), "dp").astype(jnp.float32),
        lax.psum(down_weight_sum.astype(jnp.bfloat16), "dp").astype(jnp.float32),
        lax.psum(down_bias_sum.astype(jnp.bfloat16), "dp").astype(jnp.float32),
    )
    back_attn = (
        lax.all_gather(attn_gain, "fsdp", axis=0, tiled=True),
        lax.all_gather(attn_shift, "fsdp", axis=0, tiled=True),
        lax.all_gather(heads_weight, "fsdp", axis=0, tiled=True),
        lax.all_gather(heads_bias, "fsdp", axis=0, tiled=True),
        lax.all_gather(proj_weight, "fsdp", axis=0, tiled=True),
        lax.all_gather(proj_bias, "fsdp", axis=0, tiled=True),
    )
    branch_low = grad_resid.astype(jnp.bfloat16)
    proj_bias_part = jnp.sum(branch_low.astype(jnp.float32), axis=0)
    proj_weight_part = jnp.einsum(
        "rd,re->de", heads_out, branch_low, preferred_element_type=jnp.float32
    )
    grad_heads = jnp.einsum(
        "re,de->rd", branch_low, back_attn[4], preferred_element_type=jnp.float32
    ).astype(jnp.bfloat16)
    grad_query, grad_key, grad_value = lax.map(
        attend_back,
        (queries, key_side, values, keep_groups, log_total, grad_heads.reshape(block_shape)),
    )
    grad_query = grad_query.reshape(row_count, width)
    grad_value = grad_value.reshape(row_count, width)
    grad_projected = jnp.concatenate(
        [grad_query, grad_key.reshape(row_count, width), grad_value], axis=1
    )
    heads_bias_part = jnp.concatenate(
        [
            jnp.sum(grad_query.astype(jnp.float32), axis=0),
            jnp.sum(grad_value.astype(jnp.float32), axis=0),
        ]
    )
    heads_weight_part = jnp.einsum(
        "rd,rc->dc", low_one, grad_projected, preferred_element_type=jnp.float32
    )
    grad_one = jnp.einsum(
        "rc,dc->rd", grad_projected, back_attn[2], preferred_element_type=jnp.float32
    )
    grad_entries, attn_gain_part, attn_shift_part = norm_back(
        entries, back_attn[0].astype(jnp.float32), back_attn[1].astype(jnp.float32), grad_one
    )
    tokens_grad = (grad_resid + grad_entries).astype(jnp.bfloat16)
    (
        attn_gain_sum,
        attn_shift_sum,
        heads_weight_sum,
        heads_bias_sum,
        proj_weight_sum,
        proj_bias_sum,
    ) = (
        lax.psum_scatter(
            attn_gain_part.astype(jnp.bfloat16), "fsdp", scatter_dimension=0, tiled=True
        ).astype(jnp.float32),
        lax.psum_scatter(
            attn_shift_part.astype(jnp.bfloat16), "fsdp", scatter_dimension=0, tiled=True
        ).astype(jnp.float32),
        lax.psum_scatter(
            heads_weight_part.astype(jnp.bfloat16), "fsdp", scatter_dimension=0, tiled=True
        ).astype(jnp.float32),
        lax.psum_scatter(
            heads_bias_part.astype(jnp.bfloat16), "fsdp", scatter_dimension=0, tiled=True
        ).astype(jnp.float32),
        lax.psum_scatter(
            proj_weight_part.astype(jnp.bfloat16), "fsdp", scatter_dimension=0, tiled=True
        ).astype(jnp.float32),
        lax.psum_scatter(
            proj_bias_part.astype(jnp.bfloat16), "fsdp", scatter_dimension=0, tiled=True
        ).astype(jnp.float32),
    )
    (
        attn_gain_sum,
        attn_shift_sum,
        heads_weight_sum,
        heads_bias_sum,
        proj_weight_sum,
        proj_bias_sum,
    ) = (
        lax.psum(attn_gain_sum.astype(jnp.bfloat16), "dp").astype(jnp.float32),
        lax.psum(attn_shift_sum.astype(jnp.bfloat16), "dp").astype(jnp.float32),
        lax.psum(heads_weight_sum.astype(jnp.bfloat16), "dp").astype(jnp.float32),
        lax.psum(heads_bias_sum.astype(jnp.bfloat16), "dp").astype(jnp.float32),
        lax.psum(proj_weight_sum.astype(jnp.bfloat16), "dp").astype(jnp.float32),
        lax.psum(proj_bias_sum.astype(jnp.bfloat16), "dp").astype(jnp.float32),
    )
    return (
        block_out,
        tokens_grad,
        attn_gain_sum,
        attn_shift_sum,
        heads_weight_sum,
        heads_bias_sum,
        proj_weight_sum,
        proj_bias_sum,
        mlp_gain_sum,
        mlp_shift_sum,
        up_weight_sum,
        up_bias_sum,
        down_weight_sum,
        down_bias_sum,
    )


def solution(mesh):
    return jax.shard_map(
        shards,
        mesh=mesh,
        in_specs=(
            P(("dp", "fsdp"), None),
            P(("dp", "fsdp"), None),
            P(("dp", "fsdp")),
            P(("dp", "fsdp")),
            P("fsdp"),
            P("fsdp"),
            P("fsdp", None),
            P("fsdp"),
            P("fsdp", None),
            P("fsdp"),
            P("fsdp"),
            P("fsdp"),
            P("fsdp", None),
            P("fsdp"),
            P("fsdp", None),
            P("fsdp"),
        ),
        out_specs=(
            P(("dp", "fsdp"), None),
            P(("dp", "fsdp"), None),
            P("fsdp"),
            P("fsdp"),
            P("fsdp", None),
            P("fsdp"),
            P("fsdp", None),
            P("fsdp"),
            P("fsdp"),
            P("fsdp"),
            P("fsdp", None),
            P("fsdp"),
            P("fsdp", None),
            P("fsdp"),
        ),
        check_vma=False,
    )
```

profile of v0, /device:TPU:0, one launch (start us, length us, event | category | flops | bytes accessed | tf_op | source)
XLA Modules:
  0.0 530.4 jit_solution(10582240970890792334)
XLA Ops:
  20.7 26.0 %all-reduce.16 = (bf16[1536]{0:T(1024)(128)(2,1)S(1)}, bf16[768]{0:T(1024)(128)(2,1)S(1)}, bf16[768]{0:T(1024)(128)(2,1)S(1)}, bf16[768]{0:T(1024)(128)(2,1)S(1)...) all-reduce(bf16[1536]{0:T(1024)(128)(2,1)S(1)} %dynamic-update-slic, ...), channel_id=1, replica_groups=mesh['dp'=4,'fsdp'=8] {'fsdp'}, use_global_device_ids=true, to_apply=%add.2 | all-reduce | flops 5376 | bytes 21504
  46.7 8.0 %all-gather = bf16[8,1,384]{2,1,0:T(2,128)(2,1)S(1)} all-gather(bf16[1,1,384]{2,1,0:T(2,128)(2,1)S(1)} %reshape.250), channel_id=1, replica_groups=mesh['dp'=4,'fsdp'=8] {'fsdp'}, dimensions={0}, use_global_device_ids=true | all-gather | bytes 6912 | tf_op jit(solution)/shard_map/all_gather | solution.py:141
  54.7 1.8 copy.82
  59.7 6.3 %fusion.81 = f32[1024,2304]{1,0:T(8,128)S(1)} fusion(bf16[768,2304]{1,0:T(8,128)(2,1)} %all-gather.6.cloned.1.call-done, bf16[1024,768]{0,1:T(8,128)(2,1)S(1)} %copy.82, f32[768]{0:T(1024)S(1)} %convert_element_type.201, f32[768]{0:T(1024)S(1)} %convert_element_type.200, f32[1024]{0:T(1024)S(1)} %fusion.76, f32[1024]{0:T(1024)S(1)} %broadcast_multiply_fusion.1), kind=kOutput, calls=%fused_computation.129 | convolution fusion | flops 3628597248 | bytes 14563328 | tf_op jit(solution)/shard_map/dot_general | solution.py:119
  66.1 2.3 fusion.68
  68.4 1.7 copy.84
  70.2 2.4 reshape.222
  75.8 3.9 reshape.223
  81.3 2.7 copy.83
  84.0 3.8 reshape.221
  87.8 2.8 copy.86
  90.6 2.4 broadcast.157.clone2
  92.9 15.7 %while.26 = (s32[]{:T(128)}, bf16[2,2,256,16,48]{2,1,0,4,3:T(2,128)(2,1)}, f32[2,2,16,256]{3,2,1,0:T(8,128)S(1)}, bf16[2,2,256,16,48]{2,4,3,1,0:T(8,128)(2,1)}, ...) while((s32[]{:T(128)}, ...), condition=%wide.region_5.6_spmd, body=%wide.region_2.5_spmd.sunk | while | flops 421912576 | bytes 49025728 | solution.py:131
  96.5 2.2 fusion.127
  104.2 2.2 fusion.127
  108.6 3.8 reshape.224
  112.4 3.9 fusion.89
  116.4 1.7 copy-done.2
  118.5 11.1 %fusion.83 = f32[1024,3072]{1,0:T(8,128)} fusion(bf16[768,3072]{1,0:T(8,128)(2,1)} %all-gather.10.cloned.1.call-done, f32[1024,768]{0,1:T(8,128)} %copy-done.2, f32[768]{0:T(1024)S(1)} %convert_element_type.208, f32[768]{0:T(1024)S(1)} %convert_element_type.207, f32[1024]{0:T(1024)S(1)} %fusion.77, f32[1024]{0:T(1024)S(1)} %broadcast_multiply_fusion), kind=kOutput, calls=%fused_computation.130 | convolution fusion | flops 4835770368 | bytes 20461568 | tf_op jit(solution)/shard_map/dot_general | solution.py:148
  129.6 24.7 %all-gather.12.cloned.1.call-done = bf16[3072,768]{1,0:T(8,128)(2,1)} async-done(((bf16[384,768]{1,0:T(8,128)(2,1)}), bf16[3072,768]{1,0:T(8,128)(2,1)}) %all-gather.12.cloned.1.call-update) | async-done | bytes 4718608 | tf_op jit(solution)/shard_map/all_gather | solution.py:142
  154.4 27.7 %fusion.92 = (bf16[3072]{0:T(1024)(128)(2,1)}, bf16[1024,3072]{1,0:T(8,128)(2,1)S(1)}) fusion(f32[1024,3072]{1,0:T(8,128)} %fusion.83, f32[3072]{0:T(1024)S(1)} %bitcast.140, bf16[3072,768]{1,0:T(8,128)(2,1)} %all-gather.12.cloned.1.call-done, bf16[1024,768]{0,1:T(8,128)(2,1)} %copy.91, pred[1024]{0:T(1024)(128)(4,1)S(1)} %and.34), kind=kOutput, calls=%fused_computation.138 | convolution fusion | flops 4903400448 | bytes 25185280 | tf_op jit(solution)/shard_map/rd,fd->rf/dot_general | solution.py:171
  182.1 7.4 %fusion.91 = (bf16[768]{0:T(1024)(128)(2,1)}, f32[1024,768]{1,0:T(8,128)}) fusion(bf16[1024,3072]{1,0:T(8,128)(2,1)S(1)} %get-tuple-element.292, bf16[768,3072]{1,0:T(8,128)(2,1)S(1)} %copy-done.25), kind=kOutput, calls=%fused_computation.137 | convolution fusion | flops 4832623616 | bytes 14157312 | tf_op jit(solution)/shard_map/rf,df->rd/dot_general | solution.py:179
  189.4 3.6 copy.92
  193.0 4.5 multiply_reduce_fusion.1
  201.5 2.4 convolution_convert_fusion.5
  204.0 4.3 convolution_convert_fusion.4
  208.3 3.0 copy.93
  211.3 3.9 reshape.225
  215.2 2.4 broadcast.157.clone
  217.6 30.3 %while.27 = (s32[]{:T(128)}, bf16[2,2,256,16,48]{2,4,3,1,0:T(8,128)(2,1)}, bf16[2,2,256,16,48]{2,1,0,4,3:T(2,128)(2,1)}, bf16[2,2,256,16,48]{2,4,3,1,0:T(8,128)(...) while((s32[]{:T(128)}, ...), condition=%wide.region_12.13_spmd, body=%wide.region_10.12_spmd.sunk | while | flops 1033363456 | bytes 118200152 | solution.py:228
  217.6 1.7 constant_dynamic-slice_fusion.2
  220.7 1.7 fusion.138
  222.4 2.8 multiply_reduce_fusion.5
  225.2 2.4 multiply_convert_fusion.6
  232.7 1.7 constant_dynamic-slice_fusion.2
  235.9 1.7 fusion.138
  237.6 2.8 multiply_reduce_fusion.5
  240.4 2.4 multiply_convert_fusion.6
  247.9 3.9 reshape.227
  251.8 2.8 copy.100
  254.5 4.0 reshape.228
  258.5 2.8 copy.98
  261.3 2.9 reshape.226
  265.7 2.2 copy-done.30
  268.0 5.7 %convolution_convert_fusion.3 = bf16[768,2304]{1,0:T(8,128)(2,1)} fusion(bf16[1024,2304]{0,1:T(8,128)(2,1)S(1)} %constant_dynamic-update-slice_fusion, bf16[1024,768]{0,1:T(8,128)(2,1)S(1)} %copy-done.1, f32[768]{0:T(1024)S(1)} %copy-done.47, f32[768]{0:T(1024)S(1)} %copy-done.36, f32[1024]{0:T(1024)S(1)} %copy-done.38, f32[1024]{0:T(1024)S(1)} %copy-done.34), kind=kOutput, calls=%fused_computation.70 | convolution fusion | flops 3630366720 | bytes 9844736 | tf_op jit(solution)/shard_map/rd,rc->dc/dot_general | solution.py:243
  275.1 13.0 %convolution_convert_fusion.1 = bf16[3072,768]{1,0:T(8,128)(2,1)} fusion(bf16[1024,768]{0,1:T(8,128)(2,1)S(1)} %copy-done.12, pred[1024]{0:T(1024)(128)(4,1)S(1)} %and.34, f32[1024,3072]{1,0:T(8,128)} %fusion.83, f32[3072]{0:T(1024)S(1)} %bitcast.141), kind=kOutput, calls=%fused_computation.68 | convolution fusion | flops 4868014080 | bytes 18887680 | tf_op jit(solution)/shard_map/rf,rd->fd/dot_general | solution.py:168
  288.8 9.7 %convolution_convert_fusion.2 = bf16[768,3072]{1,0:T(8,128)(2,1)} fusion(bf16[1024,3072]{1,0:T(8,128)(2,1)} %copy-done.50, f32[1024,768]{0,1:T(8,128)} %copy-done.2, f32[768]{0:T(1024)S(1)} %copy-done.32, f32[768]{0:T(1024)S(1)} %convert_element_type.207, f32[1024]{0:T(1024)S(1)} %fusion.77, f32[1024]{0:T(1024)S(1)} %broadcast_multiply_fusion), kind=kOutput, calls=%fused_computation.69 | convolution fusion | flops 4838129664 | bytes 14170112 | tf_op jit(solution)/shard_map/rd,rf->df/dot_general | solution.py:176
  301.0 1.7 reduce.5
  302.8 1.7 reduce.4
  304.6 9.1 %fusion.90 = (bf16[768]{0:T(1024)(128)(2,1)S(1)}, f32[1024,768]{1,0:T(8,128)}) fusion(bf16[1024,2304]{0,1:T(8,128)(2,1)} %copy-done.30, bf16[768,2304]{1,0:T(8,128)(2,1)} %all-gather.6.cloned.1.call-done), kind=kOutput, calls=%fused_computation.136 | convolution fusion | flops 3624664320 | bytes 11404800 | tf_op jit(solution)/shard_map/rc,dc->rd/dot_general | solution.py:246
  313.7 3.6 copy.101
  317.2 2.6 fusion.66
  321.9 2.9 add_convert_fusion
  324.8 2.7 copy.105
  327.6 23.8 %all-reduce.15 = (bf16[768]{0:T(1024)(128)(2,1)S(1)}, bf16[768]{0:T(1024)(128)(2,1)S(1)}, bf16[768]{0:T(1024)(128)(2,1)S(1)}, bf16[1536]{0:T(1024)(128)(2,1)S(1)...) all-reduce(bf16[768]{0:T(1024)(128)(2,1)S(1)} %dynamic-update-slice, ...), channel_id=1, replica_groups=mesh['dp'=4,'fsdp'=8] {'fsdp'}, use_global_device_ids=true, to_apply=%add.6 | all-reduce | flops 9984 | bytes 39936
  351.9 12.0 %all-reduce.17 = (bf16[96]{0:T(256)(128)(2,1)S(1)}, bf16[96]{0:T(256)(128)(2,1)S(1)}, bf16[192]{0:T(256)(128)(2,1)S(1)}, bf16[96]{0:T(256)(128)(2,1)S(1)}, bf16[...) all-reduce(bf16[96]{0:T(256)(128)(2,1)S(1)} %dynamic-slice.8, ...), channel_id=1, replica_groups=mesh['dp'=4,'fsdp'=8] {'dp'}, use_global_device_ids=true, to_apply=%region_17.18 | all-reduce | flops 1152 | bytes 4608 | tf_op jit(solution)/shard_map/psum | solution.py:288
  368.2 11.4 %reduce-scatter.11.cloned.1.call-done = bf16[384,768]{1,0:T(8,128)(2,1)} async-done(((bf16[3072,768]{1,0:T(8,128)(2,1)}), bf16[384,768]{1,0:T(8,128)(2,1)}) %reduce-scatter.11.cloned.1.call-update) | async-done | bytes 589840 | tf_op jit(solution)/shard_map/reduce_scatter | solution.py:197
  379.6 57.4 %reduce-scatter.9.cloned.1.call-done = bf16[96,3072]{1,0:T(8,128)(2,1)} async-done(((bf16[768,3072]{1,0:T(8,128)(2,1)}), bf16[96,3072]{1,0:T(8,128)(2,1)}) %reduce-scatter.9.cloned.1.call-update) | async-done | bytes 589840 | tf_op jit(solution)/shard_map/reduce_scatter | solution.py:191
  437.0 11.8 %select_convert_fusion = bf16[1024,768]{0,1:T(8,128)(2,1)} fusion(f32[1024,768]{0,1:T(8,128)S(1)} %copy-done.4, bf16[3072,768]{1,0:T(8,128)(2,1)} %all-gather.12.cloned.1.call-done, f32[768]{0:T(1024)S(1)} %convert_element_type.212, pred[1024]{0:T(1024)(128)(4,1)S(1)} %and.34, f32[1024,3072]{1,0:T(8,128)} %fusion.83, f32[3072]{0:T(1024)S(1)} %bitcast.142), kind=kOutput, calls=%fused_computation.100 | convolution fusion | flops 4866441216 | bytes 22036480 | tf_op jit(solution)/shard_map/dot_general | solution.py:153
  448.9 2.6 copy.104
  451.4 65.1 %all-reduce.21.cloned.1.call-done = (bf16[96,2304]{1,0:T(8,128)(2,1)}, bf16[96,768]{1,0:T(8,128)(2,1)}, bf16[96,3072]{1,0:T(8,128)(2,1)}, bf16[384,768]{1,0:T(8,128)(2,1)}) async-done(((bf16[96,2304]{1,0:T(8,128)(2,1)}, bf16[96,768]{1,0:T(8,128)(2,1)}, bf16[96,3072]{1,0:T(8,128)(2,1)}, bf16[384,768]{1,0:T(8,128)(2,1)}), (bf16[96,2304]{1,0:T(8,128)(2,1)}, bf16[96,768]{1,0:T(8,128)(2,1)}, ...) | async-done | bytes 1769488 | tf_op jit(solution)/shard_map/psum | solution.py:290
  516.5 1.7 convert_element_type.230
  518.2 2.0 convert_element_type.225
  520.2 2.2 convert_element_type.237
  (241 shorter events, 60.8 us)
Async XLA Ops:
  7.2 52.5 %all-gather.6.cloned.1.call-start = ((), (), s32[]{:S(2)}) async-start(), calls=%async_computation.4 | async-start | bytes 3981312 | tf_op jit(solution)/shard_map/all_gather | solution.py:110
  7.9 104.5 %all-gather.8.cloned.1.call-start = ((), (), s32[]{:S(2)}) async-start(), calls=%async_computation.5 | async-start | bytes 1327104 | tf_op jit(solution)/shard_map/all_gather | solution.py:112
  8.7 109.8 %all-gather.10.cloned.1.call-start = ((), (), s32[]{:S(2)}) async-start(), calls=%async_computation.6 | async-start | bytes 5308416 | tf_op jit(solution)/shard_map/all_gather | solution.py:140
  9.4 145.0 %all-gather.12.cloned.1.call-start = ((), (), s32[]{:S(2)}) async-start(), calls=%async_computation.7 | async-start | bytes 5308416 | tf_op jit(solution)/shard_map/all_gather | solution.py:142
  10.0 358.2 %reduce-scatter.7.cloned.1.call-start = ((), (), s32[]{:S(2)}) async-start(), calls=%async_computation.9 | async-start | bytes 1327104 | tf_op jit(solution)/shard_map/reduce_scatter | solution.py:273
  46.6 13.0 %copy-start.35 = (f32[768]{0:T(1024)}, f32[768]{0:T(1024)S(1)}, u32[]{:S(2)}) copy-start(f32[768]{0:T(1024)S(1)} %convert_element_type.200) | copy-start | bytes 9220
  46.6 13.0 %copy-start.46 = (f32[768]{0:T(1024)}, f32[768]{0:T(1024)S(1)}, u32[]{:S(2)}) copy-start(f32[768]{0:T(1024)S(1)} %convert_element_type.201) | copy-start | bytes 9220
  46.7 71.8 %copy-start.31 = (f32[768]{0:T(1024)}, f32[768]{0:T(1024)S(1)}, u32[]{:S(2)}) copy-start(f32[768]{0:T(1024)S(1)} %convert_element_type.208) | copy-start | bytes 9220
  54.7 3.2 copy-start.26
  56.6 3.1 copy-start
  56.9 9.1 %copy-start.33 = (f32[1024]{0:T(1024)}, f32[1024]{0:T(1024)S(1)}, u32[]{:S(2)}) copy-start(f32[1024]{0:T(1024)S(1)} %broadcast_multiply_fusion.1) | copy-start | bytes 12292
  57.9 8.0 %copy-start.37 = (f32[1024]{0:T(1024)}, f32[1024]{0:T(1024)S(1)}, u32[]{:S(2)}) copy-start(f32[1024]{0:T(1024)S(1)} %fusion.76) | copy-start | bytes 12292
  94.8 1.6 copy-start.9
  96.5 2.2 copy-start.23
  99.8 1.1 copy-start.24
  102.5 1.6 copy-start.9
  104.2 2.2 copy-start.23
  107.5 1.1 copy-start.24
  116.3 1.7 copy-start.2
  154.4 27.7 %copy-start.25 = (bf16[768,3072]{1,0:T(8,128)(2,1)S(1)}, bf16[768,3072]{1,0:T(8,128)(2,1)}, u32[]{:S(2)}) copy-start(bf16[768,3072]{1,0:T(8,128)(2,1)} %all-gather.10.cloned.1.call-done) | copy-start | bytes 14155780
  182.1 7.4 %copy-start.50 = (bf16[1024,3072]{1,0:T(8,128)(2,1)}, bf16[1024,3072]{1,0:T(8,128)(2,1)S(1)}, u32[]{:S(2)}) copy-start(bf16[1024,3072]{1,0:T(8,128)(2,1)S(1)} %get-tuple-element.292) | copy-start | bytes 18874372
  193.0 4.5 copy-start.3
  193.0 4.7 copy-start.6
  197.7 1.4 copy-start.11
  198.5 1.9 copy-start.7
  198.5 1.8 copy-start.41
  199.1 2.4 copy-start.27
  200.3 1.1 copy-start.28
  203.9 164.3 %reduce-scatter.5.cloned.1.call-start = ((), (), s32[]{:S(2)}) async-start(), calls=%async_computation.8 | async-start | bytes 3981312 | tf_op jit(solution)/shard_map/reduce_scatter | solution.py:267
  219.3 1.4 copy-start.13
  220.7 1.7 copy-start.10
  222.4 2.8 copy-start.14
  227.6 1.4 copy-start.16
  229.0 1.4 copy-start.21
  234.4 1.4 copy-start.13
  235.9 1.7 copy-start.10
  237.6 2.8 copy-start.14
  242.8 1.4 copy-start.16
  244.2 1.4 copy-start.21
  247.9 3.9 copy-start.15
  251.8 6.7 %copy-start.18 = (bf16[2,2,256,16,48]{2,4,3,1,0:T(8,128)(2,1)S(1)}, bf16[2,2,256,16,48]{2,4,3,1,0:T(8,128)(2,1)}, u32[]{:S(2)}) copy-start(bf16[2,2,256,16,48]{2,4,3,1,0:T(8,128)(2,1)} %get-tuple-element.108) | copy-start | bytes 4718596
  261.3 3.1 copy-start.19
  264.2 1.4 copy-start.20
  264.4 3.6 copy-start.1
  264.4 3.6 copy-start.34
  264.4 3.6 copy-start.36
  264.4 3.6 copy-start.38
  264.4 3.6 copy-start.47
  265.7 2.2 copy-start.30
  273.7 1.4 copy-start.12
  273.7 105.9 %reduce-scatter.11.cloned.1.call-start = ((), (), s32[]{:S(2)}) async-start(), calls=%async_computation.11 | async-start | bytes 5308416 | tf_op jit(solution)/shard_map/reduce_scatter | solution.py:197
  288.1 148.9 %reduce-scatter.9.cloned.1.call-start = ((), (), s32[]{:S(2)}) async-start(), calls=%async_computation.10 | async-start | bytes 5308416 | tf_op jit(solution)/shard_map/reduce_scatter | solution.py:191
  298.5 2.0 copy-start.49
  298.5 218.0 %all-reduce.21.cloned.1.call-start = ((), (), s32[]{:S(2)}) async-start(), calls=%async_computation.12 | async-start | bytes 3538944 | tf_op jit(solution)/shard_map/psum | solution.py:290
  317.2 2.6 copy-start.40
  317.2 2.9 copy-start.5
  319.9 2.0 copy-start.8
  319.9 2.0 copy-start.42
  324.8 2.8 copy-start.43
  324.8 2.8 copy-start.44
  324.8 2.8 copy-start.45
  324.8 2.8 copy-start.48
  324.8 112.3 %copy-start.4 = (f32[1024,768]{0,1:T(8,128)S(1)}, f32[1024,768]{0,1:T(8,128)}, u32[]{:S(2)}) copy-start(f32[1024,768]{0,1:T(8,128)} %copy-done.2) | copy-start | bytes 9437188
  516.5 5.9 %copy-start.29 = (bf16[384,768]{1,0:T(8,128)(2,1)S(1)}, bf16[384,768]{1,0:T(8,128)(2,1)}, u32[]{:S(2)}) copy-start(bf16[384,768]{1,0:T(8,128)(2,1)} %get-tuple-element.268) | copy-start | bytes 1769476
  (6 other events, 5.8 us)
Sparse Core Ops, SparseCore 0:
  9.9 36.8 all-gather.5
  48.7 24.0 all-gather.7
  74.7 38.9 all-gather.9
  115.4 38.9 all-gather.11
  204.1 36.7 reduce-scatter.6
  273.8 48.0 reduce-scatter.4
  325.7 53.8 reduce-scatter.10
  383.1 53.8 reduce-scatter.8
  439.9 76.5 all-reduce.20
where the time goes:
time: 541 us; the launch traced here: 530 us
  waiting for transfers between devices  161 us (30%)
  matrix products  136 us (25%)
  local copies, waits for them, and re-layouts  103 us (19%)
  blocking collectives  69.8 us (13%)
  other arithmetic  41 us (8%)
  between operations  18.1 us (3%)
    psum x1, waiting for transfers between devices, shards(): lax.psum(heads_weight_sum.astype(jnp.bfloat16), 'dp').astype(jnp.float32)  65.1 us
    reduce_scatter x1, waiting for transfers between devices, shards(): lax.psum_scatter(up_weight_part.astype(jnp.bfloat16), 'fsdp', scatter_dim...  57.4 us
    unnamed x2, blocking collectives  49.7 us
    dot_general x1, matrix products, shards(): jnp.einsum('rd,fd->rf', grad_out_low, back_mlp[4], preferred_element_type...  27.7 us
    unnamed x112, local copies, waits for them, and re-layouts  27.3 us
    all_gather x1, waiting for transfers between devices, shards(): lax.all_gather(down_weight, 'fsdp', axis=0, tiled=True)  24.7 us
    dot_general x1, matrix products, shards(): jnp.einsum('rf,rd->fd', active, grad_out_low, preferred_element_type=jnp....  13 us
    psum x1, blocking collectives, shards(): lax.psum(attn_gain_sum.astype(jnp.bfloat16), 'dp').astype(jnp.float32)  12 us
  transfers between devices with their start and end apart: 9, of which 4 were waited for; matrix products, arithmetic and copies ran while one was open for 39% of the time, Pallas kernels for 0%

commit v1 on v0

v1 whole, which is shorter than its diff:
```python
import functools, math
import jax, jax.numpy as jnp
from jax import lax
from jax.experimental import pallas as pl
from jax.experimental.pallas import tpu as pltpu
from jax.sharding import PartitionSpec as P

HEADS = 16
EPS = 1e-6
NEG = -1e30
F32, BF16 = jnp.float32, jnp.bfloat16
NN = (((1,), (0,)), ((), ()))
NT = (((1,), (1,)), ((), ()))
TN = (((0,), (0,)), ((), ()))

def dot(a, b, kind):
    return lax.dot_general(a, b, kind, preferred_element_type=F32)

A_GAIN, A_SHIFT, P_BIAS, M_GAIN, M_SHIFT, D_BIAS, H_BIAS, U_BIAS = 0, 1, 2, 3, 4, 5, 6, 8
SQ = math.sqrt(2.0 / math.pi)

def norm_stats(x):
    mean = jnp.mean(x, axis=-1, keepdims=True)
    cen = x - mean
    var = jnp.mean(cen * cen, axis=-1, keepdims=True)
    rstd = lax.rsqrt(var + EPS)
    return cen * rstd, rstd

def loop(n, body):
    def step(i, c):
        body(i)
        return c
    lax.fori_loop(0, n, step, 0)

def ds(i, size):
    return pl.ds(pl.multiple_of(i * size, size), size)

def keep_rows(top_ref, rows_ref, img, shape):
    grid_row = lax.broadcasted_iota(jnp.int32, shape, 0)
    lo = top_ref[img] * 16
    hi = lo + rows_ref[img] * 16
    return jnp.logical_and(grid_row >= lo, grid_row < hi)

def head_spans(h):
    a, b = 48 * h, 48 * h + 48
    t0, t1 = a // 128, (b - 1) // 128
    if t0 == t1:
        return [(t0, a - 128 * t0, b - 128 * t0)]
    return [(t0, a - 128 * t0, 128), (t1, 0, b - 128 * t1)]

def head_tools(h, lane):
    spans = head_spans(h)
    def inside(lo, hi):
        return jnp.logical_and(lane >= lo, lane < hi)
    masks = [(t, inside(lo, hi)) for t, lo, hi in spans]
    mh = masks[0][1]
    for t, m in masks[1:]:
        mh = jnp.logical_or(mh, m)
    used = set()
    for t, lo, hi in spans:
        used |= set(range(lo, hi))
    free = [l for l in range(128) if l not in used][:4]
    def window(tiles):
        if len(spans) == 1:
            return tiles[spans[0][0]]
        return jnp.where(masks[0][1], tiles[spans[0][0]], tiles[spans[1][0]])
    return masks, mh, free, window

def split3(v):
    hi = v.astype(BF16)
    r = v - hi.astype(F32)
    mid = r.astype(BF16)
    lo = (r - mid.astype(F32)).astype(BF16)
    return hi, mid, lo

def attn_fwd(t, top_ref, rows_ref, qkv, qx, ho):
    img, half = t // 2, t % 2
    rows = ds(img, 256)
    def cols(base, j):
        return pl.ds(pl.multiple_of(half * 384 + base + 128 * j, 128), 128)
    q = [qkv[rows, cols(0, j)] for j in range(3)]
    k = [qkv[rows, cols(768, j)] for j in range(3)]
    v = [qkv[rows, cols(1536, j)] for j in range(3)]
    lane = lax.broadcasted_iota(jnp.int32, (256, 128), 1)
    bias = jnp.where(keep_rows(top_ref, rows_ref, img, (256, 128)), 0.0, NEG).astype(BF16)
    out = [jnp.zeros((256, 128), F32) for _ in range(3)]
    ones = jnp.ones((256, 128), BF16)
    zero, one = jnp.zeros((256, 128), BF16), jnp.ones((256, 128), BF16)
    for h in range(8):
        masks, mh, free, window = head_tools(h, lane)
        qw, kw, vw = window(q), window(k), window(v)
        qi = jnp.where(mh, qw, jnp.where(lane == free[0], one, zero))
        ki = jnp.where(lane == free[0], bias, kw)
        s = dot(qi, ki, NT)
        m = jnp.max(s, axis=1, keepdims=True)
        e = jnp.exp(s - m).astype(BF16)
        res = dot(e, jnp.concatenate([vw, ones], axis=1), NN)
        o, tot = res[:, :128], res[:, 128:]
        o = o / tot
        for j, mk in masks:
            out[j] = jnp.where(mk, o, out[j])
        lse = m + jnp.log(tot)
        hi, mid, lo = split3(-lse)
        ext = jnp.where(lane == free[1], hi, jnp.where(lane == free[2], mid, jnp.where(lane == free[3], lo, zero)))
        ext = jnp.where(lane == free[0], one, ext)
        qx[rows, pl.ds(pl.multiple_of(half * 1024 + 128 * h, 128), 128)] = jnp.where(mh, qw, ext)
    for j in range(3):
        ho[rows, cols(0, j)] = out[j].astype(BF16)

def attn_bwd(img, half, top_ref, rows_ref, qkv, qx, ho, gh, factor):
    rows = ds(img, 256)
    def cols(base, j):
        return pl.ds(pl.multiple_of(half * 384 + base + 128 * j, 128), 128)
    k = [qkv[rows, cols(768, j)] for j in range(3)]
    v = [qkv[rows, cols(1536, j)] for j in range(3)]
    o = [ho[rows, cols(0, j)] for j in range(3)]
    do = [gh[rows, cols(0, j)] for j in range(3)]
    lane = lax.broadcasted_iota(jnp.int32, (256, 128), 1)
    bias = jnp.where(keep_rows(top_ref, rows_ref, img, (256, 128)), 0.0, NEG).astype(BF16)
    zero, one = jnp.zeros((256, 128), BF16), jnp.ones((256, 128), BF16)
    dq = [jnp.zeros((256, 128), F32) for _ in range(3)]
    dk = [jnp.zeros((256, 128), F32) for _ in range(3)]
    dv = [jnp.zeros((256, 128), F32) for _ in range(3)]
    for h in range(8):
        masks, mh, free, window = head_tools(h, lane)
        kw, vw, ow, dow = window(k), window(v), window(o), window(do)
        qw = qx[rows, pl.ds(pl.multiple_of(half * 1024 + 128 * h, 128), 128)]
        ki = jnp.where(mh, kw, jnp.where(lane == free[0], bias, one))
        pt = jnp.exp(dot(ki, qw, NT))
        prod = jnp.where(mh, dow.astype(F32) * ow.astype(F32), 0.0)
        dd = jnp.broadcast_to(jnp.sum(prod, axis=1, keepdims=True), (256, 128))
        hi, mid, lo = split3(-dd)
        di = jnp.where(mh, dow, jnp.where(lane == free[1], hi, jnp.where(lane == free[2], mid, jnp.where(lane == free[3], lo, zero))))
        vi = jnp.where(mh, vw, one)
        dpt = dot(vi, di, NT)
        dst = (pt * dpt).astype(BF16)
        rv = dot(pt.astype(BF16), dow, NN)
        rk = dot(dst, qw, NN)
        rq = dot(dst, kw, TN) * factor
        for j, mk in masks:
            dq[j] = jnp.where(mk, rq, dq[j])
            dk[j] = jnp.where(mk, rk, dk[j])
            dv[j] = jnp.where(mk, rv, dv[j])
    for j in range(3):
        qkv[rows, cols(0, j)] = dq[j].astype(BF16)
        qkv[rows, cols(768, j)] = dk[j].astype(BF16)
        qkv[rows, cols(1536, j)] = dv[j].astype(BF16)

def st_norm1(tok, par, low1):
    def body(i):
        x = tok[ds(i, 256), :].astype(F32)
        xh, _ = norm_stats(x)
        low1[ds(i, 256), :] = (xh * par[A_GAIN:A_GAIN + 1, :] + par[A_SHIFT:A_SHIFT + 1, :]).astype(BF16)
    loop(4, body)

def st_mask(cot, top_ref, rows_ref, acc):
    def body(i):
        keep = keep_rows(top_ref, rows_ref, i, (256, 768))
        g = jnp.where(keep, cot[ds(i, 256), :].astype(F32), 0.0)
        acc[D_BIAS:D_BIAS + 1, :] += jnp.sum(g, axis=0, keepdims=True)
        cot[ds(i, 256), :] = g.astype(BF16)
    loop(4, body)

def st_qkv(n, low1, wqkv, par, qkv, factor):
    cols = slice(768 * n, 768 * n + 768)
    def body(i):
        p = dot(low1[ds(i, 256), :], wqkv[:, cols], NN)
        if n == 0:
            p = (p + par[H_BIAS:H_BIAS + 1, :]) * factor
        if n == 2:
            p = p + par[H_BIAS + 1:H_BIAS + 2, :]
        qkv[ds(i, 256), cols] = p.astype(BF16)
    loop(4, body)

def st_proj(ho, wp, tok, par, resid, low2):
    def body(i):
        rows = ds(i, 256)
        r = tok[rows, :].astype(F32) + (dot(ho[rows, :], wp[...], NN) + par[P_BIAS:P_BIAS + 1, :])
        resid[rows, :] = r
        xh, _ = norm_stats(r)
        low2[rows, :] = (xh * par[M_GAIN:M_GAIN + 1, :] + par[M_SHIFT:M_SHIFT + 1, :]).astype(BF16)
    loop(4, body)

def st_up(n, low2, wu, par, act, gp):
    cols = slice(768 * n, 768 * n + 768)
    def body(i):
        rows = ds(i, 256)
        z = dot(low2[rows, :], wu[:, cols], NN) + par[U_BIAS + n:U_BIAS + n + 1, :]
        z2 = z * z
        t = jnp.tanh(z * (SQ + (SQ * 0.044715) * z2))
        hz = 0.5 * z
        act[rows, cols] = (hz + hz * t).astype(BF16)
        gp[rows, cols] = (0.5 + 0.5 * t + hz * (1.0 - t * t) * (SQ + (3 * SQ * 0.044715) * z2)).astype(BF16)
    loop(4, body)

def st_down(act, wd, par, resid, top_ref, rows_ref, out):
    def body(i):
        rows = ds(i, 256)
        r = resid[rows, :] + (dot(act[rows, :], wd[...], NN) + par[D_BIAS:D_BIAS + 1, :])
        keep = keep_rows(top_ref, rows_ref, i, (256, 768))
        out[rows, :] = jnp.where(keep, r, 0.0).astype(BF16)
    loop(4, body)

def st_dwd(n, act, g, dwd):
    cols = slice(256 * n, 256 * n + 256)
    def body(i):
        dwd[ds(i, 768), cols] = dot(act[:, ds(i, 768)], g[:, cols], TN).astype(BF16)
    loop(4, body)

def st_gact(n, g, wd, gp, acc):
    cols = slice(768 * n, 768 * n + 768)
    def body(i):
        rows = ds(i, 256)
        ga = dot(g[rows, :], wd[cols, :], NT)
        gh = (ga * gp[rows, cols].astype(F32)).astype(BF16)
        acc[U_BIAS + n:U_BIAS + n + 1, :] += jnp.sum(gh.astype(F32), axis=0, keepdims=True)
        gp[rows, cols] = gh
    loop(4, body)

def st_dwu(n, low2, gh, dwu):
    cols = slice(768 * n, 768 * n + 768)
    def body(i):
        dwu[ds(i, 256), :] = dot(low2[:, ds(i, 256)], gh[:, cols], TN).astype(BF16)
    loop(3, body)

def st_gtwo(gh, wu, par, resid, g, acc, branch):
    def body(i):
        rows = ds(i, 256)
        gt = dot(gh[rows, :], wu[...], NT)
        xh, rstd = norm_stats(resid[rows, :])
        acc[M_GAIN:M_GAIN + 1, :] += jnp.sum(gt * xh, axis=0, keepdims=True)
        acc[M_SHIFT:M_SHIFT + 1, :] += jnp.sum(gt, axis=0, keepdims=True)
        u = gt * par[M_GAIN:M_GAIN + 1, :]
        m1 = jnp.mean(u, axis=1, keepdims=True)
        m2 = jnp.mean(u * xh, axis=1, keepdims=True)
        gr = g[rows, :].astype(F32) + (u - m1 - xh * m2) * rstd
        resid[rows, :] = gr
        b = gr.astype(BF16)
        acc[P_BIAS:P_BIAS + 1, :] += jnp.sum(b.astype(F32), axis=0, keepdims=True)
        branch[rows, :] = b
    loop(4, body)

def st_dwp(ho, branch, dwp):
    def body(i):
        dwp[ds(i, 256), :] = dot(ho[:, ds(i, 256)], branch[...], TN).astype(BF16)
    loop(3, body)

def st_gheads(branch, wp, gheads):
    def body(i):
        gheads[ds(i, 256), :] = dot(branch[ds(i, 256), :], wp[...], NT).astype(BF16)
    loop(4, body)

def st_hbias(qkv, acc):
    def body(i):
        rows = ds(i, 256)
        acc[H_BIAS:H_BIAS + 1, :] += jnp.sum(qkv[rows, 0:768].astype(F32), axis=0, keepdims=True)
        acc[H_BIAS + 1:H_BIAS + 2, :] += jnp.sum(qkv[rows, 1536:2304].astype(F32), axis=0, keepdims=True)
    loop(4, body)

def st_dwqkv(low1, dqkv, dw, ncol, base):
    def body(i):
        dw[ds(i, 256), base:base + ncol] = dot(low1[:, ds(i, 256)], dqkv[:, base:base + ncol], TN).astype(BF16)
    loop(3, body)

def st_gone(dqkv, wqkv, tok, par, gres, acc, out):
    def body(i):
        rows = ds(i, 256)
        go = dot(dqkv[rows, :], wqkv[...], NT)
        xh, rstd = norm_stats(tok[rows, :].astype(F32))
        acc[A_GAIN:A_GAIN + 1, :] += jnp.sum(go * xh, axis=0, keepdims=True)
        acc[A_SHIFT:A_SHIFT + 1, :] += jnp.sum(go, axis=0, keepdims=True)
        u = go * par[A_GAIN:A_GAIN + 1, :]
        m1 = jnp.mean(u, axis=1, keepdims=True)
        m2 = jnp.mean(u * xh, axis=1, keepdims=True)
        out[rows, :] = (gres[rows, :] + (u - m1 - xh * m2) * rstd).astype(BF16)
    loop(4, body)


def compute_kernel(top_ref, rows_ref, tok_h, cot_h, par, wqkv_h, wp_h, wu_h, wd_h,
                   out_h, tg_h, dwqkv_h, dwp_h, dwu_h, dwd_h, acc,
                   tok, cot, low1, qkv, qx, ho, resid, low2, act, gp, wqkv, wp, wu, wd, dwd, sems):
    factor = 1.0 / math.sqrt(768 // HEADS)
    cps = [pltpu.make_async_copy(s, d, sems.at[i]) for i, (s, d) in enumerate(
        ((tok_h, tok), (wqkv_h, wqkv), (wp_h, wp), (wu_h, wu), (cot_h, cot), (wd_h, wd)))]
    for c in cps:
        c.start()
    acc[...] = jnp.zeros_like(acc)
    cps[0].wait()
    st_norm1(tok, par, low1)
    cps[1].wait()
    for n in range(3):
        st_qkv(n, low1, wqkv, par, qkv, factor)
    loop(8, lambda t: attn_fwd(t, top_ref, rows_ref, qkv, qx, ho))
    cps[2].wait()
    st_proj(ho, wp, tok, par, resid, low2)
    cps[3].wait()
    for n in range(4):
        st_up(n, low2, wu, par, act, gp)
    cps[4].wait()
    st_mask(cot, top_ref, rows_ref, acc)
    for n in range(3):
        st_dwd(n, act, cot, dwd)
    cps[5].wait()
    stage = act.at[:, 0:768]
    gheads = act.at[:, 768:1536]
    st_down(act, wd, par, resid, top_ref, rows_ref, stage)
    o1 = pltpu.make_async_copy(stage, out_h, sems.at[6]); o1.start()
    o2 = pltpu.make_async_copy(dwd, dwd_h, sems.at[7]); o2.start()
    for n in range(4):
        st_gact(n, cot, wd, gp, acc)
    outs = [o2]
    for n in range(4):
        dst = wd.at[768 * n:768 * n + 768, :]
        st_dwu(n, low2, gp, dst)
        o = pltpu.make_async_copy(dst, dwu_h.at[n], sems.at[8 + n]); o.start()
        outs.append(o)
    st_gtwo(gp, wu, par, resid, cot, acc, low2)
    dwp = wu.at[:, 0:768]
    st_dwp(ho, low2, dwp)
    o = pltpu.make_async_copy(dwp, dwp_h, sems.at[12]); o.start()
    outs.append(o)
    st_gheads(low2, wp, gheads)
    dwqkv = wu.at[:, 768:3072]
    for half in range(2):
        loop(4, lambda img: attn_bwd(img, half, top_ref, rows_ref, qkv, qx, ho, gheads, factor))
    st_hbias(qkv, acc)
    for n in range(3):
        st_dwqkv(low1, qkv, dwqkv, 768, 768 * n)
    o = pltpu.make_async_copy(dwqkv, dwqkv_h, sems.at[13]); o.start()
    outs.append(o)
    o1.wait()
    st_gone(qkv, wqkv, tok, par, resid, acc, stage)
    o = pltpu.make_async_copy(stage, tg_h, sems.at[14]); o.start()
    outs.append(o)
    for o in outs:
        o.wait()


def compute_call(crop_top, crop_rows, tokens, cotangent, par, wqkv, wp, wu, wd):
    R = tokens.shape[0]
    sds = jax.ShapeDtypeStruct
    anyspec = pl.BlockSpec(memory_space=pl.ANY)
    v = pltpu.VMEM
    return pl.pallas_call(
        compute_kernel,
        out_shape=(sds((R, 768), BF16), sds((R, 768), BF16), sds((768, 2304), BF16), sds((768, 768), BF16),
                   sds((4, 768, 768), BF16), sds((3072, 768), BF16), sds((16, 768), F32)),
        in_specs=[pl.BlockSpec(memory_space=pltpu.SMEM)] * 2 + [anyspec] * 2 + [pl.BlockSpec(memory_space=v)] + [anyspec] * 4,
        out_specs=[anyspec] * 6 + [pl.BlockSpec(memory_space=v)],
        scratch_shapes=[v((R, 768), BF16), v((R, 768), BF16), v((R, 768), BF16), v((R, 2304), BF16), v((R, 2048), BF16),
                        v((R, 768), BF16), v((R, 768), F32), v((R, 768), BF16), v((R, 3072), BF16), v((R, 3072), BF16),
                        v((768, 2304), BF16), v((768, 768), BF16), v((768, 3072), BF16), v((3072, 768), BF16),
                        v((3072, 768), BF16), pltpu.SemaphoreType.DMA((16,))],
        compiler_params=pltpu.CompilerParams(vmem_limit_bytes=60 * 2**20),
        cost_estimate=pl.CostEstimate(flops=46 * 10**9, bytes_accessed=40 * 10**6, transcendentals=12 * 10**6),
    )(crop_top, crop_rows, tokens, cotangent, par, wqkv, wp, wu, wd)


def pack_small(ag, ash, hb, pb, mg, ms, ub, db):
    n = ag.shape[0]
    return jnp.concatenate(
        [jnp.stack([ag, ash, pb, mg, ms, db]), hb.reshape(2, n), ub.reshape(4, n), jnp.zeros((4, n), ag.dtype)]
    ).astype(F32)


def small_table(parts):
    s, _, n = parts.shape
    six = parts[:, :6].transpose(1, 0, 2).reshape(6, s * n)
    hb = parts[:, 6:8].reshape(2, s * n)
    ub = parts[:, 8:12].reshape(4, s * n)
    return jnp.concatenate([six, hb, ub, jnp.zeros((4, s * n), F32)])


def small_pieces(acc, s):
    n = acc.shape[1] // s
    six = acc[:6].reshape(6, s, n).transpose(1, 0, 2)
    hb = acc[6:8].reshape(s, 2, n)
    ub = acc[8:12].reshape(s, 4, n)
    return jnp.concatenate([six, hb, ub, jnp.zeros((s, 4, n), F32)], axis=1)


def shards(tokens, cotangent, crop_rows, crop_top, ag, ash, hw, hb, pw, pb, mg, ms, uw, ub, dw, db):
    def gather(a):
        return lax.all_gather(a, "fsdp", axis=0, tiled=True)

    def reduce(a):
        part = lax.psum_scatter(a.astype(BF16), "fsdp", scatter_dimension=0, tiled=True)
        return lax.psum(part, "dp").astype(F32)

    s = lax.axis_size("fsdp")
    par = small_table(lax.all_gather(pack_small(ag, ash, hb, pb, mg, ms, ub, db), "fsdp", axis=0))
    out, tg, dwqkv, dwp, dwu, dwd, acc = compute_call(
        crop_top, crop_rows, tokens, cotangent, par, gather(hw), gather(pw), gather(uw), gather(dw))
    dwu = dwu.transpose(1, 0, 2).reshape(uw.shape[0] * s, -1)
    small = small_pieces(acc, s)
    small = lax.psum(lax.psum_scatter(small, "fsdp", scatter_dimension=0, tiled=True), "dp")[0]
    return (out, tg, small[0], small[1], reduce(dwqkv), small[6:8].reshape(-1), reduce(dwp), small[2],
            small[3], small[4], reduce(dwu), small[8:12].reshape(-1), reduce(dwd), small[5])


def solution(mesh):
    row = P(("dp", "fsdp"), None)
    vec, mat = P("fsdp"), P("fsdp", None)
    return jax.shard_map(
        shards,
        mesh=mesh,
        in_specs=(row, row, P(("dp", "fsdp")), P(("dp", "fsdp")), vec, vec, mat, vec, mat, vec, vec, vec, mat, vec, mat, vec),
        out_specs=(row, row, vec, vec, mat, vec, mat, vec, vec, vec, mat, vec, mat, vec),
        check_vma=False,
    )
```

time: 541 us -> 622 us (1.15); the launches traced: 530 us -> 621 us
  waiting for transfers between devices: 161 us -> 442 us
  matrix products: 136 us -> 0 us
  Pallas kernels: 0 us -> 113 us
  local copies, waits for them, and re-layouts: 103 us -> 22.8 us
  blocking collectives: 69.8 us -> 22.7 us
  other arithmetic: 41 us -> 6.18 us
    dot_general x26 -> x0, matrix products: 136 us -> none  [the longest x1 27.7 us: shards(): jnp.einsum('rd,fd->rf', grad_out_low, back_mlp[4], preferred_element_type...]
    reduce_scatter x4, waiting for transfers between devices: 68.8 us -> 185 us  [the longest x3 147 us: reduce(): lax.psum_scatter(a.astype(BF16), 'fsdp', scatter_dimension=0, tiled=True)]
    pallas_call x0 -> x1, Pallas kernels: none -> 113 us  [compute_call(): pl.pallas_call(compute_kernel, out_shape=(sds((R, 768), BF16), sds((R, 76...]
    all_gather x4, waiting for transfers between devices: 24.8 us -> 130 us  [gather(): return lax.all_gather(a, 'fsdp', axis=0, tiled=True)]
    unnamed x9 -> x11, waiting for transfers between devices: 2.66 us -> 55.3 us
    unnamed x2 -> x0, blocking collectives: 49.7 us -> none
    reshape x8 -> x9, local copies, waits for them, and re-layouts: 28.5 us -> 1.82 us  [the longest x1 0.66 us: shards(): small[8:12].reshape(-1)]
    reduce_sum x12 -> x0, other arithmetic: 18.3 us -> none  [the longest x3 8.44 us: layer_norm(): return centered * lax.rsqrt(spread + EPSILON) * norm_gain + norm_shift]
  transfers between devices with their start and end apart: 9 -> 10, of which waited for: 4 -> 10; matrix products, arithmetic and copies ran while one was open for 39% -> 1% of each run, Pallas kernels for 0% -> 0%
where the time goes in v1:
time: 622 us; the launch traced here: 621 us
  waiting for transfers between devices  442 us (71%)
  Pallas kernels  113 us (18%)
  local copies, waits for them, and re-layouts  22.8 us (4%)
  blocking collectives  22.7 us (4%)
  between operations  14.3 us (2%)
    reduce_scatter x3, waiting for transfers between devices, reduce(): lax.psum_scatter(a.astype(BF16), 'fsdp', scatter_dimension=0, tiled=True)  147 us
    all_gather x4, waiting for transfers between devices, gather(): return lax.all_gather(a, 'fsdp', axis=0, tiled=True)  130 us
    pallas_call x1, Pallas kernels, compute_call(): pl.pallas_call(compute_kernel, out_shape=(sds((R, 768), BF16), sds((R, 76...  113 us
    psum x1, waiting for transfers between devices, reduce(): return lax.psum(part, 'dp').astype(F32)  72.2 us
    unnamed x11, waiting for transfers between devices  55.3 us
    reduce_scatter x1, waiting for transfers between devices, shards(): lax.psum_scatter(small, 'fsdp', scatter_dimension=0, tiled=True)  37.1 us
  transfers between devices with their start and end apart: 10, of which 10 were waited for; matrix products, arithmetic and copies ran while one was open for 1% of the time, Pallas kernels for 0%

profile of v1, /device:TPU:0, one launch (start us, length us, event | category | flops | bytes accessed | tf_op | source)
XLA Modules:
  0.0 621.3 jit_solution(6220510824624372109)
XLA Ops:
  7.2 0.0 all-gather.7.cloned.1.call-start
  7.2 0.7 all-gather.7.cloned.1.call-update
  7.9 0.0 all-gather.5.cloned.1.call-start
  8.0 0.7 all-gather.5.cloned.1.call-update
  8.7 0.0 all-gather.9.cloned.1.call-start
  8.7 0.7 all-gather.9.cloned.1.call-update
  9.4 0.0 all-gather.11.cloned.1.call-start
  9.4 0.5 all-gather.11.cloned.1.call-update
  10.0 0.0 reduce-scatter.16.cloned.1.call-start
  10.0 0.7 concatenate.38
  10.8 0.8 concatenate.39
  11.5 0.8 concatenate.40
  12.3 10.7 %all_gather.16 = f32[8,16,96]{2,1,0:T(8,128)S(1)} all-gather(f32[1,16,96]{2,1,0:T(8,128)S(1)} %convert_element_type.22), channel_id=1, replica_groups=mesh['dp'=4,'fsdp'=8] {'fsdp'}, dimensions={0}, use_global_device_ids=true | all-gather | bytes 55296 | tf_op jit(solution)/shard_map/all_gather | solution.py:391
  23.0 0.1 reshape.196
  23.1 0.1 reshape.197
  23.2 0.1 reshape.195
  23.3 0.1 pad.7.clone
  23.4 0.7 maximum_maximum_fusion.1.par
  24.1 12.6 %all-gather.7.cloned.1.call-done.wp_h = bf16[768,768]{1,0:T(8,128)(2,1)} async-done(((bf16[96,768]{1,0:T(8,128)(2,1)}), bf16[768,768]{1,0:T(8,128)(2,1)}) %all-gather.7.cloned.1.call-update) | async-done | bytes 1179664 | tf_op jit(solution)/shard_map/all_gather | solution.py:384
  36.7 35.9 %all-gather.5.cloned.1.call-done.wqkv_h = bf16[768,2304]{1,0:T(8,128)(2,1)} async-done(((bf16[96,2304]{1,0:T(8,128)(2,1)}), bf16[768,2304]{1,0:T(8,128)(2,1)}) %all-gather.5.cloned.1.call-update) | async-done | bytes 3538960 | tf_op jit(solution)/shard_map/all_gather | solution.py:384
  72.6 40.8 %all-gather.9.cloned.1.call-done.wu_h = bf16[768,3072]{1,0:T(8,128)(2,1)} async-done(((bf16[96,3072]{1,0:T(8,128)(2,1)}), bf16[768,3072]{1,0:T(8,128)(2,1)}) %all-gather.9.cloned.1.call-update) | async-done | bytes 4718608 | tf_op jit(solution)/shard_map/all_gather | solution.py:384
  113.4 40.7 %all-gather.11.cloned.1.call-done.wd_h = bf16[3072,768]{1,0:T(8,128)(2,1)} async-done(((bf16[384,768]{1,0:T(8,128)(2,1)}), bf16[3072,768]{1,0:T(8,128)(2,1)}) %all-gather.11.cloned.1.call-update) | async-done | bytes 4718608 | tf_op jit(solution)/shard_map/all_gather | solution.py:384
  154.1 112.8 %shard_map.263 = (bf16[1024,768]{1,0:T(8,128)(2,1)}, bf16[1024,768]{1,0:T(8,128)(2,1)}, bf16[768,2304]{1,0:T(8,128)(2,1)}, bf16[768,768]{1,0:T(8,128)(2,1)}, bf1...) custom-call(s32[4]{0:T(128)} %top_ref.1, s32[4]{0:T(128)} %rows_ref.1, ...), custom_call_target="tpu_custom_call" | custom-call | flops 46000001024 | bytes 40000000 | tf_op jit(solution)/shard_map/pallas_call | solution.py:344
  266.9 6.6 %copy.38 = bf16[768,4,768]{0,2,1:T(8,128)(2,1)} copy(bf16[768,4,768]{2,0,1:T(8,128)(2,1)} %bitcast.27) | data formatting | bytes 9437184 | tf_op jit(solution)/shard_map/transpose | solution.py:394
  273.6 6.7 %copy.40 = bf16[768,3072]{1,0:T(8,128)(2,1)} copy(bf16[768,3072]{0,1:T(8,128)(2,1)} %bitcast.26) | data formatting | bytes 9437184
  280.3 0.0 reduce-scatter.16.cloned.1.call-update
  280.3 0.0 reduce-scatter.12.cloned.1.call-start
  280.4 0.5 reduce-scatter.12.cloned.1.call-update
  280.9 0.0 reduce-scatter.10.cloned.1.call-start
  280.9 0.0 copy-start.1
  280.9 0.7 reduce-scatter.10.cloned.1.call-update
  281.6 0.0 reduce-scatter.14.cloned.1.call-start
  281.7 0.7 reduce-scatter.14.cloned.1.call-update
  282.4 0.0 reduce-scatter.8.cloned.1.call-start
  282.4 0.0 copy-done.1
  282.5 0.1 reshape.199
  282.6 0.1 reshape.198
  282.6 0.1 reshape.200
  282.7 0.7 maximum_maximum_fusion
  283.5 0.0 reduce-scatter.8.cloned.1.call-update
  283.5 0.0 all-reduce.3.cloned.1.call-start
  283.5 50.8 %reduce-scatter.16.cloned.1.call-done = bf16[96,3072]{1,0:T(8,128)(2,1)} async-done(((bf16[768,3072]{1,0:T(8,128)(2,1)}), bf16[96,3072]{1,0:T(8,128)(2,1)}) %reduce-scatter.16.cloned.1.call-update) | async-done | bytes 589840
  334.3 2.2 copy.41
  336.6 38.6 %reduce-scatter.12.cloned.1.call-done = bf16[96,768]{1,0:T(8,128)(2,1)} async-done(((bf16[768,768]{1,0:T(8,128)(2,1)}), bf16[96,768]{1,0:T(8,128)(2,1)}) %reduce-scatter.12.cloned.1.call-update) | async-done | bytes 147472 | tf_op jit(solution)/shard_map/reduce_scatter | solution.py:387
  375.1 51.6 %reduce-scatter.10.cloned.1.call-done = bf16[96,2304]{1,0:T(8,128)(2,1)} async-done(((bf16[768,2304]{1,0:T(8,128)(2,1)}), bf16[96,2304]{1,0:T(8,128)(2,1)}) %reduce-scatter.10.cloned.1.call-update) | async-done | bytes 442384 | tf_op jit(solution)/shard_map/reduce_scatter | solution.py:387
  426.7 57.3 %reduce-scatter.14.cloned.1.call-done = bf16[384,768]{1,0:T(8,128)(2,1)} async-done(((bf16[3072,768]{1,0:T(8,128)(2,1)}), bf16[384,768]{1,0:T(8,128)(2,1)}) %reduce-scatter.14.cloned.1.call-update) | async-done | bytes 589840 | tf_op jit(solution)/shard_map/reduce_scatter | solution.py:387
  484.0 0.0 all-reduce.3.cloned.1.call-update
  484.1 37.1 %reduce-scatter.8.cloned.1.call-done = f32[1,16,96]{2,1,0:T(8,128)} async-done(((f32[8,16,96]{2,1,0:T(8,128)}), f32[1,16,96]{2,1,0:T(8,128)}) %reduce-scatter.8.cloned.1.call-update) | async-done | bytes 6160 | tf_op jit(solution)/shard_map/reduce_scatter | solution.py:396
  521.2 12.1 %psum.35 = f32[1,16,96]{2,1,0:T(8,128)S(1)} all-reduce(f32[1,16,96]{2,1,0:T(8,128)} %reduce-scatter.8.cloned.1.call-done), channel_id=1, replica_groups=mesh['dp'=4,'fsdp'=8] {'dp'}, use_global_device_ids=true, to_apply=%region_1.0 | all-reduce | flops 1536 | bytes 12288 | tf_op jit(solution)/shard_map/psum | solution.py:396
  533.3 0.6 reshape.201
  533.9 0.7 reshape.203
  534.6 0.5 slice_bitcast_fusion.1
  535.1 72.2 %all-reduce.3.cloned.1.call-done = (bf16[96,3072]{0,1:T(8,128)(2,1)}, bf16[96,2304]{1,0:T(8,128)(2,1)}, bf16[96,768]{1,0:T(8,128)(2,1)}, bf16[384,768]{1,0:T(8,128)(2,1)}) async-done(((bf16[96,3072]{0,1:T(8,128)(2,1)}, bf16[96,2304]{1,0:T(8,128)(2,1)}, bf16[96,768]{1,0:T(8,128)(2,1)}, bf16[384,768]{1,0:T(8,128)(2,1)}), (bf16[96,3072]{0,1:T(8,128)(2,1)}, bf16[96,2304]{1,0:T(8,128)(2,1)}, ...) | async-done | bytes 1769488 | tf_op jit(solution)/shard_map/psum | solution.py:388
  607.3 0.0 copy-start
  607.3 1.7 convert_element_type.24
  609.0 2.4 copy.39
  611.4 2.0 convert_element_type.23
  613.4 0.0 copy-done
  613.4 1.1 convert_element_type.26
  (13 shorter events, 0.1 us)
Async XLA Ops:
  7.2 29.5 %all-gather.7.cloned.1.call-start = ((), (), s32[]{:S(2)}) async-start(), calls=%async_computation.6 | async-start | bytes 1327104 | tf_op jit(solution)/shard_map/all_gather | solution.py:384
  7.9 64.7 %all-gather.5.cloned.1.call-start = ((), (), s32[]{:S(2)}) async-start(), calls=%async_computation.5 | async-start | bytes 3981312 | tf_op jit(solution)/shard_map/all_gather | solution.py:384
  8.7 104.8 %all-gather.9.cloned.1.call-start = ((), (), s32[]{:S(2)}) async-start(), calls=%async_computation.7 | async-start | bytes 5308416 | tf_op jit(solution)/shard_map/all_gather | solution.py:384
  9.4 144.7 %all-gather.11.cloned.1.call-start = ((), (), s32[]{:S(2)}) async-start(), calls=%async_computation.8 | async-start | bytes 5308416 | tf_op jit(solution)/shard_map/all_gather | solution.py:384
  10.0 324.4 %reduce-scatter.16.cloned.1.call-start = ((), (), s32[]{:S(2)}) async-start(), calls=%async_computation.13 | async-start | bytes 5308416
  280.3 94.8 %reduce-scatter.12.cloned.1.call-start = ((), (), s32[]{:S(2)}) async-start(), calls=%async_computation.11 | async-start | bytes 1327104 | tf_op jit(solution)/shard_map/reduce_scatter | solution.py:387
  280.9 145.8 %reduce-scatter.10.cloned.1.call-start = ((), (), s32[]{:S(2)}) async-start(), calls=%async_computation.10 | async-start | bytes 3981312 | tf_op jit(solution)/shard_map/reduce_scatter | solution.py:387
  280.9 1.5 copy-start.1
  281.6 202.4 %reduce-scatter.14.cloned.1.call-start = ((), (), s32[]{:S(2)}) async-start(), calls=%async_computation.12 | async-start | bytes 5308416 | tf_op jit(solution)/shard_map/reduce_scatter | solution.py:387
  282.4 238.8 %reduce-scatter.8.cloned.1.call-start = ((), (), s32[]{:S(2)}) async-start(), calls=%async_computation.9 | async-start | bytes 73728 | tf_op jit(solution)/shard_map/reduce_scatter | solution.py:396
  283.5 323.8 %all-reduce.3.cloned.1.call-start = ((), (), s32[]{:S(2)}) async-start(), calls=%async_computation.14 | async-start | bytes 3932160 | tf_op jit(solution)/shard_map/psum | solution.py:388
  607.3 6.1 copy-start
Sparse Core Ops, SparseCore 0:
  9.9 26.7 all-gather.6
  38.6 33.9 all-gather.4
  74.5 38.9 all-gather.8
  115.2 38.9 all-gather.10
  280.4 53.8 reduce-scatter.15
  338.3 36.7 reduce-scatter.11
  378.6 48.0 reduce-scatter.9
  430.1 53.8 reduce-scatter.13
  487.9 33.2 reduce-scatter.7
  524.2 83.0 all-reduce.2
